TPU v7x, 128 devices: a whole 4x4x4 slice. The times are simulated.
128 devices in a mesh: gx: 4 (over x_lo, core), gy: 4 (over y), gz: 8 (over x_hi, z).
Axes of the slice: x: 4 (x_hi: 2, x_lo: 2; x = x_hi * 2 + x_lo), y: 4, z: 4, core: 2. Of those that a mesh axis runs over, the one named last changes fastest.
Arguments:
- positions: float32 [3, 2048, 128], P(None, ('gx', 'gy', 'gz')), may hold values from -6 to 6
- velocities: float32 [3, 2048, 128], P(None, ('gx', 'gy', 'gz')), may hold values from -6 to 6
- weights: float32 [2048, 128], P(('gx', 'gy', 'gz')), may hold values from 0.5 to 2
- counts: int32 [2048], P(('gx', 'gy', 'gz')), may hold values from 32 to 128
- link_offset: int32 [2048, 3], P(('gx', 'gy', 'gz')), may hold values from -16 to 16
- link_mask: int32 [2048, 3], P(('gx', 'gy', 'gz')), may hold values 0 or 1
- bin_box: int32 [2048, 1], P(('gx', 'gy', 'gz')), may hold values from 0 to 15; in each aligned block of 16 rows (0 to 15, 16 to 31, ...) at most 2 rows name the same one
- bin_cell: int32 [2048], P(('gx', 'gy', 'gz')), may hold values from 0 to 4095
- fluid: float32 [3, 16, 32, 1024], P(None, 'gx', 'gy', 'gz'), may hold values from -6 to 6
Outputs:
- positions_out: float32 [3, 2048, 128], P(None, ('gx', 'gy', 'gz'))
- velocities_out: float32 [3, 2048, 128], P(None, ('gx', 'gy', 'gz'))
- fluid_out: float32 [3, 16, 32, 1024], P(None, 'gx', 'gy', 'gz')
Inputs may be any that keep to these rules, and one draw needn't show every extreme that they name: `bin_box`: the bins of one device name one value at most 2 times; the cell lies in the box at the bin owner's index of gz. `bin_cell`: index of the cell inside its box, first dimension slowest. Slots 0 to counts - 1 of a bin are occupied.
All inputs are finite; a program needn't handle non-finite values. No bound on the sum of `link_mask` on one device may be relied on, other than what follows from the above.
Results may differ from a plain program's by a relative error of at most 0.0001.
Values sent between devices are 32-bit elements; how exact they have to be, the bound alone decides.
A program may use at most 128 MiB of HBM per device.

v0:
```python
import jax
import jax.numpy as jnp
from jax import lax
from jax.sharding import PartitionSpec as P

SUBSTEPS = 2
step_sub = 0.1
stiffness = 0.05
damping = 0.05
drag_rate = 1.0
coupling = 0.004
viscosity = 0.12
highest = lax.Precision.HIGHEST


def padded_2(cells, sides, width):
    for axis, dim in sides:
        count = lax.axis_size(axis)
        ends = count - 1
        head = lax.slice_in_dim(cells, 0, width, axis=dim)
        tail = lax.slice_in_dim(cells, cells.shape[dim] - width, cells.shape[dim], axis=dim)
        cells = jnp.concatenate(
            [
                lax.ppermute(tail, axis, [(i, (i + 1) % count) for i in range(ends)]),
                cells,
                lax.ppermute(head, axis, [((i + 1) % count, i) for i in range(ends)]),
            ],
            axis=dim,
        )
    return cells


def contact(own_pos, own_vel, near_pos, near_vel, near_weight):
    distance = jnp.zeros(
        near_weight.shape[:2] + (own_pos.shape[2], near_weight.shape[2]), jnp.float32
    )
    for component in range(3):
        offset = own_pos[component][:, None, :, None] - near_pos[component][:, :, None, :]
        distance = distance + offset * offset
    kernel = near_weight[:, :, None, :] * jnp.exp(-0.5 * distance)
    weight_sum = jnp.sum(kernel, axis=(1, 3))
    pull_pos = jnp.einsum("bqij,cbqj->cbi", kernel, near_pos, precision=highest)
    pull_vel = jnp.einsum("bqij,cbqj->cbi", kernel, near_vel, precision=highest)
    return stiffness * (own_pos * weight_sum[None] - pull_pos) - damping * (
        own_vel * weight_sum[None] - pull_vel
    )


def advance(
    widened, state_pos, state_vel, carried, occupied, fluid_seen, neighbour, link_weight, block_bins
):
    bin_count = state_pos.shape[1]

    def one_block(block_id, running):
        nearby = widened[:, neighbour]
        near_pos = jnp.concatenate([state_pos[:, :, None], nearby[0:3]], 2)
        near_vel = jnp.concatenate([state_vel[:, :, None], nearby[3:6]], 2)
        near_weight = jnp.concatenate([carried[:, None], nearby[6] * link_weight[:, :, None]], 1)
        contact_force = contact(state_pos, state_vel, near_pos, near_vel, near_weight)
        drag_force = drag_rate * (fluid_seen[:, :, None] - state_vel)
        moved_vel = state_vel + step_sub * occupied[None] * (contact_force + drag_force)
        moved_pos = state_pos + step_sub * occupied[None] * moved_vel
        pulled_block = jnp.sum(carried[None] * drag_force, axis=2)
        return (moved_pos, moved_vel, pulled_block)

    start_state = (
        jnp.zeros_like(state_pos),
        jnp.zeros_like(state_vel),
        jnp.zeros((3, bin_count), jnp.float32),
    )
    return lax.fori_loop(0, bin_count // block_bins, one_block, start_state)


def stencil(padded):
    centre = padded[:, 1:-1, 1:-1, 1:-1]
    beside_all = padded[:, 2:, 1:-1, 1:-1] + padded[:, :-2, 1:-1, 1:-1]
    beside_all = beside_all + padded[:, 1:-1, 2:, 1:-1] + padded[:, 1:-1, :-2, 1:-1]
    beside_all = beside_all + padded[:, 1:-1, 1:-1, 2:] + padded[:, 1:-1, 1:-1, :-2]
    return beside_all - 6.0 * centre


def local(positions, velocities, weights, counts, link_offset, link_mask, bin_box, bin_cell, fluid):
    bin_count = positions.shape[1]
    slot_count = positions.shape[2]
    cell_count = fluid.shape[1] * fluid.shape[2] * fluid.shape[3]
    flat_fluid = fluid.reshape(3, cell_count)
    occupied = (
        lax.broadcasted_iota(jnp.int32, (bin_count, slot_count), 1) < counts[:, None]
    ).astype(jnp.float32)
    carried = weights * occupied
    target = bin_box[:, 0]
    box_piece = lax.all_gather(flat_fluid[None], ("gx", "gy"), axis=0, tiled=True)
    first_box = jnp.int32(0)
    local_box = jnp.clip(target, 0, box_piece.shape[0] - 1)
    inside = (target >= first_box) & (target < first_box + box_piece.shape[0])
    picked = box_piece[local_box, :, bin_cell]
    fluid_seen = jnp.where(inside[:, None], picked, 0.0).T
    neighbour = lax.broadcasted_iota(jnp.int32, (bin_count, 1), 0) + link_offset + bin_count
    link_weight = link_mask.astype(jnp.float32)
    block_bins = 16
    state_pos = positions
    state_vel = velocities
    pulled_total = jnp.zeros((3, bin_count), jnp.float32)
    for substep in range(SUBSTEPS):
        packed = jnp.concatenate([state_pos, state_vel, carried[None]], 0)
        widened = padded_2(packed, ((("gx", "gy", "gz"), 1),), bin_count)
        state_pos, state_vel, pulled = advance(
            widened,
            state_pos,
            state_vel,
            carried,
            occupied,
            fluid_seen,
            neighbour,
            link_weight,
            block_bins,
        )
        pulled_total = pulled_total + pulled
    pushed_all = -coupling * pulled_total.T
    first_box = jnp.int32(0)
    local_box = jnp.clip(target, 0, 1 * lax.axis_size(("gx", "gy")) - 1)
    inside = (target >= first_box) & (target < first_box + 1 * lax.axis_size(("gx", "gy")))
    pushed = jnp.where(inside[:, None], pushed_all, 0.0)
    source = lax.psum_scatter(
        jnp.zeros((1 * lax.axis_size(("gx", "gy")), 3, cell_count), jnp.float32)
        .at[local_box, :, bin_cell]
        .add(pushed),
        ("gx", "gy"),
        scatter_dimension=0,
        tiled=True,
    ).reshape(fluid.shape)

    def fluid_rate(velocity_field):
        padded = padded_2(velocity_field, (("gx", 1), ("gy", 2), ("gz", 3)), 1)
        return viscosity * stencil(padded) + source

    first_rate = fluid_rate(fluid)
    middle = fluid + first_rate
    second_rate = fluid_rate(middle)
    fluid_out = fluid + 0.5 * (first_rate + second_rate)
    return (state_pos, state_vel, fluid_out)


def solution(mesh):
    in_specs = (
        P(None, ("gx", "gy", "gz"), None),
        P(None, ("gx", "gy", "gz"), None),
        P(("gx", "gy", "gz"), None),
        P(("gx", "gy", "gz")),
        P(("gx", "gy", "gz"), None),
        P(("gx", "gy", "gz"), None),
        P(("gx", "gy", "gz"), None),
        P(("gx", "gy", "gz")),
        P(None, "gx", "gy", "gz"),
    )
    out_specs = (
        P(None, ("gx", "gy", "gz"), None),
        P(None, ("gx", "gy", "gz"), None),
        P(None, "gx", "gy", "gz"),
    )
    return jax.shard_map(local, mesh=mesh, in_specs=in_specs, out_specs=out_specs, check_vma=False)
```

profile of v0, /device:TPU:6, one launch (start us, length us, event | category | flops | bytes accessed | tf_op | source)
XLA Modules:
  0.0 504.4 jit_solution(973373740408308659)
XLA Ops:
  9.5 6.8 %collective-permute-start.1 = (f32[7,16,128]{2,0,1:T(8,128)S(1)}, f32[7,16,128]{2,0,1:T(8,128)S(1)}, u32[]{:S(2)}, u32[]{:S(2)}) collective-permute-start(f32[7,16,128]{2,0,1:T(8,128)S(1)} %pad_maximum_fusion.5), channel_id=1, source_target_pairs={{1,0},{2,1},{3,2},{4,3},{5,4},{6,5},{7,6},{8,7},{9,8},{10,9},{11,1... | collective-permute-start | bytes 172040 | tf_op jit(solution)/shard_map/ppermute | solution.py:26
  16.3 1.9 collective-permute-start
  19.0 1.9 collective-permute-start.5
  20.9 3.6 collective-permute-start.4
  26.1 34.2 %all_gather.3 = f32[16,3,4096]{2,1,0:T(4,128)S(1)} all-gather(f32[1,3,4096]{2,1,0:T(4,128)S(1)} %broadcast_in_dim_reshape.3), channel_id=1, replica_groups=mesh['gx'=4,'gy'=4,'gz'=8] {'gx','gy'}, dimensions={0}, use_global_device_ids=true | all-gather | bytes 835584 | tf_op jit(solution)/shard_map/all_gather | solution.py:92
  60.3 15.6 %copy.101 = f32[16,3,4096]{1,2,0:T(8,128)} copy(f32[16,3,4096]{2,1,0:T(4,128)S(1)} %all_gather.3) | data formatting | bytes 1572864 | tf_op jit(solution)/shard_map/all_gather | solution.py:92
  76.1 1.3 gather_fusion.1
  78.5 2.3 fusion.2
  80.8 5.6 %fusion.49 = f32[3,16,128]{2,0,1:T(4,128)S(1)} fusion(f32[16,4,128]{2,1,0:T(4,128)S(1)} %bitcast.141, f32[16,128]{1,0:T(8,128)S(1)} %get-tuple-element.117, f32[16,4,128]{2,1,0:T(4,128)S(1)} %bitcast.144, f32[16,128]{1,0:T(8,128)S(1)} %get-tuple-element.116, f32[16,4,128]{2,1,0:T(4,128)S(1)} %bitcast.138, f32[16,128]{1,0:T(8,128)S(1)} %get-tuple-element.115, ...), kind=kOutput, calls=%fused_computation.55 | convolution fusion | flops 48277504 | bytes 311296 | tf_op jit(solution)/shard_map/while/body/eval_jaxpr/bqij,cbqj->cbi/dot_general | solution.py:42
  86.4 5.9 %multiply_reduce_fusion = (f32[3,16]{0,1:T(8,128)S(1)}, f32[3,16]{0,1:T(8,128)S(1)}, f32[3,16,128]{2,0,1:T(4,128)S(1)}, f32[3,16,128]{2,0,1:T(4,128)S(1)}) fusion(f32[16,128]{1,0:T(8,128)S(1)} %get-tuple-element.121, f32[3,16]{0,1:T(8,128)S(1)} %select_bitcast_fusion.1, f32[3,16,128]{2,1,0:T(8,128)S(1)} %copy-done.2, ...), kind=kOutput, calls=%fused_computation.141 | convolution fusion | flops 48351136 | bytes 401984 | tf_op jit(solution)/shard_map/while/body/eval_jaxpr/bqij,cbqj->cbi/dot_general | solution.py:43
  92.4 11.0 %broadcast_in_dim.105 = f32[16,3,4096]{1,2,0:T(8,128)} broadcast(f32[]{:T(128)} %constant.18.clone.1), dimensions={} | broadcast | bytes 786436 | tf_op jit(solution)/shard_map/broadcast_in_dim | solution.py:125
  103.5 2.2 scatter_fusion
  105.7 1.3 collective-permute-start.6
  107.0 4.5 collective-permute-start.7
  111.6 1.3 collective-permute-done.7
  113.0 1.9 collective-permute-start.9
  115.0 7.5 %collective-permute-start.8 = (f32[3,6,10,1]{3,2,1,0:T(8,128)S(1)}, f32[3,6,10,1]{3,2,1,0:T(8,128)S(1)}, u32[]{:S(2)}, u32[]{:S(2)}) collective-permute-start(f32[3,6,10,1]{3,2,1,0:T(8,128)S(1)} %get-tuple-element.81), channel_id=1, source_target_pairs={{1,0},{2,1},{3,2},{4,3},{5,4},{6,5},{7,6},{9,8},{10,9},{11,10},{12... | collective-permute-start | bytes 2168 | tf_op jit(solution)/shard_map/ppermute | solution.py:26
  122.5 3.9 collective-permute-start.3
  126.5 1.9 collective-permute-start.2
  128.4 1.2 collective-permute-done.3
  129.6 6.6 %collective-permute-done.2 = f32[7,16,128]{2,0,1:T(8,128)S(1)} collective-permute-done((f32[7,16,128]{2,0,1:T(8,128)S(1)}, f32[7,16,128]{2,0,1:T(8,128)S(1)}, u32[]{:S(2)}, u32[]{:S(2)}) %collective-permute-start.2) | collective-permute-done | bytes 57376 | tf_op jit(solution)/shard_map/ppermute | solution.py:24
  137.2 321.7 %reduce-scatter.2.cloned.1.call-done = f32[1,3,4096]{1,2,0:T(8,128)} async-done(((f32[16,3,4096]{1,2,0:T(8,128)}), f32[1,3,4096]{1,2,0:T(8,128)}) %reduce-scatter.2.cloned.1.call-update) | async-done | bytes 49168 | tf_op jit(solution)/shard_map/reduce_scatter | solution.py:124
  458.9 2.2 copy.109
  461.3 2.5 collective-permute-start.10
  463.8 1.9 collective-permute-start.11
  465.7 2.2 fusion.5
  468.8 1.3 collective-permute-start.12
  470.1 4.5 collective-permute-start.13
  474.7 5.6 %fusion.57 = f32[3,16,128]{2,0,1:T(4,128)S(1)} fusion(f32[16,4,128]{2,1,0:T(4,128)S(1)} %bitcast.132, f32[16,128]{1,0:T(8,128)S(1)} %bitcast.150, f32[16,4,128]{2,1,0:T(4,128)S(1)} %bitcast.135, f32[16,128]{1,0:T(8,128)S(1)} %bitcast.153, f32[16,4,128]{2,1,0:T(4,128)S(1)} %bitcast.129, f32[16,128]{1,0:T(8,128)S(1)} %bitcast.147, ...), kind=kOutput, calls=%fused_computation.63 | convolution fusion | flops 48277504 | bytes 311296 | tf_op jit(solution)/shard_map/while/body/eval_jaxpr/bqij,cbqj->cbi/dot_general | solution.py:42
  480.4 3.4 collective-permute-start.15
  483.9 6.0 %collective-permute-start.14 = (f32[3,6,10,1]{3,2,1,0:T(8,128)S(1)}, f32[3,6,10,1]{3,2,1,0:T(8,128)S(1)}, u32[]{:S(2)}, u32[]{:S(2)}) collective-permute-start(f32[3,6,10,1]{3,2,1,0:T(8,128)S(1)} %get-tuple-element.79), channel_id=1, source_target_pairs={{1,0},{2,1},{3,2},{4,3},{5,4},{6,5},{7,6},{9,8},{10,9},{11,10},{12... | collective-permute-start | bytes 2168 | tf_op jit(solution)/shard_map/ppermute | solution.py:26
  489.9 5.6 %multiply_add_fusion = (f32[3,16,128]{2,0,1:T(4,128)S(1)}, f32[3,16,128]{2,0,1:T(4,128)S(1)}) fusion(f32[3,16,128]{2,0,1:T(4,128)S(1)} %get-tuple-element.109, f32[16,128]{1,0:T(8,128)S(1)} %get-tuple-element.120, f32[3,16,128]{2,0,1:T(4,128)S(1)} %get-tuple-element.122, f32[3,16]{0,1:T(8,128)S(1)} %select_bitcast_fusion.1, f32[3,16,128]{2,0,1:T(4,128)S(1)} %fusion.57, ...), kind=kOutput, calls=%fused_computation.143 | convolution fusion | flops 48320512 | bytes 393408 | tf_op jit(solution)/shard_map/while/body/eval_jaxpr/bqij,cbqj->cbi/dot_general | solution.py:43
  (77 shorter events, 10.2 us)
Async XLA Ops:
  7.2 451.7 %reduce-scatter.2.cloned.1.call-start = ((), (), s32[]{:S(2)}) async-start(), calls=%async_computation.1 | async-start | bytes 35651584 | tf_op jit(solution)/shard_map/reduce_scatter | solution.py:124
  9.5 68.0 %collective-permute-start.1 = (f32[7,16,128]{2,0,1:T(8,128)S(1)}, f32[7,16,128]{2,0,1:T(8,128)S(1)}, u32[]{:S(2)}, u32[]{:S(2)}) collective-permute-start(f32[7,16,128]{2,0,1:T(8,128)S(1)} %pad_maximum_fusion.5), channel_id=1, source_target_pairs={{1,0},{2,1},{3,2},{4,3},{5,4},{6,5},{7,6},{8,7},{9,8},{10,9},{11,1... | collective-permute-start | bytes 172040 | tf_op jit(solution)/shard_map/ppermute | solution.py:26
  16.3 61.3 %collective-permute-start = (f32[7,16,128]{2,0,1:T(8,128)S(1)}, f32[7,16,128]{2,0,1:T(8,128)S(1)}, u32[]{:S(2)}, u32[]{:S(2)}) collective-permute-start(f32[7,16,128]{2,0,1:T(8,128)S(1)} %pad_maximum_fusion.5), channel_id=1, source_target_pairs={{0,1},{1,2},{2,3},{3,4},{4,5},{5,6},{6,7},{7,8},{8,9},{9,10},{10,1... | collective-permute-start | bytes 172040 | tf_op jit(solution)/shard_map/ppermute | solution.py:24
  19.0 58.5 %collective-permute-start.5 = (f32[3,1,8,128]{3,2,1,0:T(8,128)S(1)}, f32[3,1,8,128]{3,2,1,0:T(8,128)S(1)}, u32[]{:S(2)}, u32[]{:S(2)}) collective-permute-start(f32[3,1,8,128]{3,2,1,0:T(8,128)S(1)} %get-tuple-element.108), channel_id=1, source_target_pairs={{0,32},{32,64},{64,96},{1,33},{33,65},{65,97},{2,34},{34,66},{66,9... | collective-permute-start | bytes 36872 | tf_op jit(solution)/shard_map/ppermute | solution.py:24
  20.9 56.6 %collective-permute-start.4 = (f32[3,1,8,128]{3,2,1,0:T(8,128)S(1)}, f32[3,1,8,128]{3,2,1,0:T(8,128)S(1)}, u32[]{:S(2)}, u32[]{:S(2)}) collective-permute-start(f32[3,1,8,128]{3,2,1,0:T(8,128)S(1)} %get-tuple-element.107), channel_id=1, source_target_pairs={{32,0},{64,32},{96,64},{33,1},{65,33},{97,65},{34,2},{66,34},{98,6... | collective-permute-start | bytes 36872 | tf_op jit(solution)/shard_map/ppermute | solution.py:26
  60.3 15.6 %copy-start.6 = (s32[16,1]{0,1:T(1,128)S(1)}, s32[16,1]{0,1:T(1,128)}, u32[]{:S(2)}) copy-start(s32[16,1]{0,1:T(1,128)} %param.15) | copy-start | bytes 196
  60.3 15.6 %copy-start.5 = (s32[16]{0:T(128)S(1)}, s32[16]{0:T(128)}, u32[]{:S(2)}) copy-start(s32[16]{0:T(128)} %param.16) | copy-start | bytes 196
  60.3 15.6 %copy-start.3 = (s32[16,3]{0,1:T(4,128)S(1)}, s32[16,3]{0,1:T(4,128)}, u32[]{:S(2)}) copy-start(s32[16,3]{0,1:T(4,128)} %param.13) | copy-start | bytes 580
  60.3 17.2 %copy-start.4 = (s32[16,3]{0,1:T(4,128)S(1)}, s32[16,3]{0,1:T(4,128)}, u32[]{:S(2)}) copy-start(s32[16,3]{0,1:T(4,128)} %param.14) | copy-start | bytes 580
  60.3 17.2 %copy-start = (f32[3,4,8,128]{3,2,1,0:T(8,128)S(1)}, f32[3,4,8,128]{3,2,1,0:T(8,128)}, u32[]{:S(2)}) copy-start(f32[3,4,8,128]{3,2,1,0:T(8,128)} %param.17) | copy-start | bytes 147460
  60.3 20.5 %copy-start.1 = (f32[3,16,128]{2,1,0:T(8,128)S(1)}, f32[3,16,128]{2,1,0:T(8,128)}, u32[]{:S(2)}) copy-start(f32[3,16,128]{2,1,0:T(8,128)} %param.9) | copy-start | bytes 73732
  80.8 5.6 %copy-start.2 = (f32[3,16,128]{2,1,0:T(8,128)S(1)}, f32[3,16,128]{2,1,0:T(8,128)}, u32[]{:S(2)}) copy-start(f32[3,16,128]{2,1,0:T(8,128)} %param.10) | copy-start | bytes 73732
  105.7 5.9 %collective-permute-start.6 = (f32[3,6,1,128]{3,2,1,0:T(1,128)S(1)}, f32[3,6,1,128]{3,2,1,0:T(1,128)S(1)}, u32[]{:S(2)}, u32[]{:S(2)}) collective-permute-start(f32[3,6,1,128]{3,2,1,0:T(1,128)S(1)} %get-tuple-element.104), channel_id=1, source_target_pairs={{8,0},{16,8},{24,16},{9,1},{17,9},{25,17},{10,2},{18,10},{26,18},{... | collective-permute-start | bytes 27656 | tf_op jit(solution)/shard_map/ppermute | solution.py:26
  107.0 5.9 %collective-permute-start.7 = (f32[3,6,1,128]{3,2,1,0:T(1,128)S(1)}, f32[3,6,1,128]{3,2,1,0:T(1,128)S(1)}, u32[]{:S(2)}, u32[]{:S(2)}) collective-permute-start(f32[3,6,1,128]{3,2,1,0:T(1,128)S(1)} %get-tuple-element.103), channel_id=1, source_target_pairs={{0,8},{8,16},{16,24},{1,9},{9,17},{17,25},{2,10},{10,18},{18,26},{... | collective-permute-start | bytes 27656 | tf_op jit(solution)/shard_map/ppermute | solution.py:24
  113.0 348.1 %collective-permute-start.9 = (f32[3,6,10,1]{3,2,1,0:T(8,128)S(1)}, f32[3,6,10,1]{3,2,1,0:T(8,128)S(1)}, u32[]{:S(2)}, u32[]{:S(2)}) collective-permute-start(f32[3,6,10,1]{3,2,1,0:T(8,128)S(1)} %get-tuple-element.82), channel_id=1, source_target_pairs={{0,1},{1,2},{2,3},{3,4},{4,5},{5,6},{6,7},{8,9},{9,10},{10,11},{11... | collective-permute-start | bytes 2168 | tf_op jit(solution)/shard_map/ppermute | solution.py:24
  115.0 346.2 %collective-permute-start.8 = (f32[3,6,10,1]{3,2,1,0:T(8,128)S(1)}, f32[3,6,10,1]{3,2,1,0:T(8,128)S(1)}, u32[]{:S(2)}, u32[]{:S(2)}) collective-permute-start(f32[3,6,10,1]{3,2,1,0:T(8,128)S(1)} %get-tuple-element.81), channel_id=1, source_target_pairs={{1,0},{2,1},{3,2},{4,3},{5,4},{6,5},{7,6},{9,8},{10,9},{11,10},{12... | collective-permute-start | bytes 2168 | tf_op jit(solution)/shard_map/ppermute | solution.py:26
  122.5 7.1 %collective-permute-start.3 = (f32[7,16,128]{2,0,1:T(8,128)S(1)}, f32[7,16,128]{2,0,1:T(8,128)S(1)}, u32[]{:S(2)}, u32[]{:S(2)}) collective-permute-start(f32[7,16,128]{2,0,1:T(8,128)S(1)} %pad_maximum_fusion.4), channel_id=1, source_target_pairs={{1,0},{2,1},{3,2},{4,3},{5,4},{6,5},{7,6},{8,7},{9,8},{10,9},{11,1... | collective-permute-start | bytes 172040 | tf_op jit(solution)/shard_map/ppermute | solution.py:26
  126.5 9.8 %collective-permute-start.2 = (f32[7,16,128]{2,0,1:T(8,128)S(1)}, f32[7,16,128]{2,0,1:T(8,128)S(1)}, u32[]{:S(2)}, u32[]{:S(2)}) collective-permute-start(f32[7,16,128]{2,0,1:T(8,128)S(1)} %pad_maximum_fusion.4), channel_id=1, source_target_pairs={{0,1},{1,2},{2,3},{3,4},{4,5},{5,6},{6,7},{7,8},{8,9},{9,10},{10,1... | collective-permute-start | bytes 172040 | tf_op jit(solution)/shard_map/ppermute | solution.py:24
  461.3 6.7 %collective-permute-start.10 = (f32[3,1,8,128]{3,2,1,0:T(8,128)S(1)}, f32[3,1,8,128]{3,2,1,0:T(8,128)S(1)}, u32[]{:S(2)}, u32[]{:S(2)}) collective-permute-start(f32[3,1,8,128]{3,2,1,0:T(8,128)S(1)} %get-tuple-element.106), channel_id=1, source_target_pairs={{32,0},{64,32},{96,64},{33,1},{65,33},{97,65},{34,2},{66,34},{98,6... | collective-permute-start | bytes 36872 | tf_op jit(solution)/shard_map/ppermute | solution.py:26
  463.8 5.0 collective-permute-start.11
  468.8 11.5 %collective-permute-start.12 = (f32[3,6,1,128]{3,2,1,0:T(1,128)S(1)}, f32[3,6,1,128]{3,2,1,0:T(1,128)S(1)}, u32[]{:S(2)}, u32[]{:S(2)}) collective-permute-start(f32[3,6,1,128]{3,2,1,0:T(1,128)S(1)} %get-tuple-element.102), channel_id=1, source_target_pairs={{8,0},{16,8},{24,16},{9,1},{17,9},{25,17},{10,2},{18,10},{26,18},{... | collective-permute-start | bytes 27656 | tf_op jit(solution)/shard_map/ppermute | solution.py:26
  470.1 10.2 %collective-permute-start.13 = (f32[3,6,1,128]{3,2,1,0:T(1,128)S(1)}, f32[3,6,1,128]{3,2,1,0:T(1,128)S(1)}, u32[]{:S(2)}, u32[]{:S(2)}) collective-permute-start(f32[3,6,1,128]{3,2,1,0:T(1,128)S(1)} %get-tuple-element.101), channel_id=1, source_target_pairs={{0,8},{8,16},{16,24},{1,9},{9,17},{17,25},{2,10},{10,18},{18,26},{... | collective-permute-start | bytes 27656 | tf_op jit(solution)/shard_map/ppermute | solution.py:24
  480.4 16.3 %collective-permute-start.15 = (f32[3,6,10,1]{3,2,1,0:T(8,128)S(1)}, f32[3,6,10,1]{3,2,1,0:T(8,128)S(1)}, u32[]{:S(2)}, u32[]{:S(2)}) collective-permute-start(f32[3,6,10,1]{3,2,1,0:T(8,128)S(1)} %get-tuple-element.80), channel_id=1, source_target_pairs={{0,1},{1,2},{2,3},{3,4},{4,5},{5,6},{6,7},{8,9},{9,10},{10,11},{11... | collective-permute-start | bytes 2168 | tf_op jit(solution)/shard_map/ppermute | solution.py:24
  483.9 12.9 %collective-permute-start.14 = (f32[3,6,10,1]{3,2,1,0:T(8,128)S(1)}, f32[3,6,10,1]{3,2,1,0:T(8,128)S(1)}, u32[]{:S(2)}, u32[]{:S(2)}) collective-permute-start(f32[3,6,10,1]{3,2,1,0:T(8,128)S(1)} %get-tuple-element.79), channel_id=1, source_target_pairs={{1,0},{2,1},{3,2},{4,3},{5,4},{6,5},{7,6},{9,8},{10,9},{11,10},{12... | collective-permute-start | bytes 2168 | tf_op jit(solution)/shard_map/ppermute | solution.py:26
Sparse Core Ops, SparseCore 0:
  105.8 353.0 reduce-scatter.1
where the time goes:
time: 505 us; the launch traced here: 504 us
  waiting for transfers between devices  332 us (66%)
  starting transfers between devices  55.1 us (11%)
  local copies, waits for them, and re-layouts  37 us (7%)
  blocking collectives  34.2 us (7%)
  matrix products  22.8 us (5%)
  between operations  14.5 us (3%)
  other arithmetic  9.07 us (2%)
    reduce_scatter x1, waiting for transfers between devices, local(): lax.psum_scatter(jnp.zeros((1 * lax.axis_size(('gx', 'gy')), 3, cell_coun...  322 us
    all_gather x1, blocking collectives, local(): lax.all_gather(flat_fluid[None], ('gx', 'gy'), axis=0, tiled=True)  34.2 us
    ppermute x8, starting transfers between devices, padded_2(): lax.ppermute(head, axis, [((i + 1) % count, i) for i in range(ends)])  33 us
    ppermute x8, starting transfers between devices, padded_2(): lax.ppermute(tail, axis, [(i, (i + 1) % count) for i in range(ends)])  22.1 us
    all_gather x1, local copies, waits for them, and re-layouts, local(): lax.all_gather(flat_fluid[None], ('gx', 'gy'), axis=0, tiled=True)  15.6 us
    dot_general x2, matrix products, contact(): pull_vel = jnp.einsum('bqij,cbqj->cbi', kernel, near_vel, precision=highest)  11.6 us
    dot_general x2, matrix products, contact(): pull_pos = jnp.einsum('bqij,cbqj->cbi', kernel, near_pos, precision=highest)  11.2 us
    broadcast_in_dim x1, local copies, waits for them, and re-layouts, local(): jnp.zeros((1 * lax.axis_size(('gx', 'gy')), 3, cell_count), jnp.float32)  11 us
  transfers between devices with their start and end apart: 17, of which 5 were waited for; matrix products, arithmetic and copies ran while one was open for 7% of the time, Pallas kernels for 0%

commit v1 on v0

--- a/solution.py
+++ b/solution.py
@@ -1,3 +1,4 @@
+import functools
 import jax
 import jax.numpy as jnp
 from jax import lax
@@ -11,6 +12,21 @@
 coupling = 0.004
 viscosity = 0.12
 highest = lax.Precision.HIGHEST
+
+
+def check_works_on(x0, mesh_name, dim_no):
+    return jnp.concatenate(
+        jax.lax.all_to_all(
+            jnp.stack([x0 for _ in range(jax.lax.axis_size(mesh_name))]),
+            axis_name=mesh_name,
+            split_axis=0,
+            concat_axis=0,
+        ),
+        axis=dim_no,
+    )
+
+
+recover_the_panel = functools.partial(check_works_on, mesh_name=("gx", "gy"), dim_no=0)
 
 
 def padded_2(cells, sides, width):
@@ -89,7 +105,7 @@
     ).astype(jnp.float32)
     carried = weights * occupied
     target = bin_box[:, 0]
-    box_piece = lax.all_gather(flat_fluid[None], ("gx", "gy"), axis=0, tiled=True)
+    box_piece = recover_the_panel(flat_fluid[None])
     first_box = jnp.int32(0)
     local_box = jnp.clip(target, 0, box_piece.shape[0] - 1)
     inside = (target >= first_box) & (target < first_box + box_piece.shape[0])

time: 505 us -> 484 us (0.958)
  blocking collectives: 34.2 us -> 0 us
  starting transfers between devices: 55.1 us -> 61.1 us
    all_gather x1 -> x0, blocking collectives: 34.2 us -> none  [local(): lax.all_gather(flat_fluid[None], ('gx', 'gy'), axis=0, tiled=True)]
    all_to_all x0 -> x1, local copies, waits for them, and re-layouts: none -> 16.1 us  [check_works_on(): jax.lax.all_to_all(jnp.stack([x0 for _ in range(jax.lax.axis_size(mesh_na...]
    all_gather x1 -> x0, local copies, waits for them, and re-layouts: 15.6 us -> none  [local(): lax.all_gather(flat_fluid[None], ('gx', 'gy'), axis=0, tiled=True)]
    all_to_all x0 -> x1, starting transfers between devices: none -> 5.95 us  [check_works_on(): jax.lax.all_to_all(jnp.stack([x0 for _ in range(jax.lax.axis_size(mesh_na...]
  transfers between devices with their start and end apart: 17 -> 18, of which waited for: 5 -> 6; matrix products, arithmetic and copies ran while one was open for 7% -> 7% of each run, Pallas kernels for 0% -> 0%
where the time goes in v1:
time: 484 us; the launch traced here: 482 us
  waiting for transfers between devices  333 us (69%)
  starting transfers between devices  61.1 us (13%)
  local copies, waits for them, and re-layouts  39.2 us (8%)
  matrix products  22.8 us (5%)
  between operations  14.5 us (3%)
  other arithmetic  11.8 us (2%)
    reduce_scatter x1, waiting for transfers between devices, local(): lax.psum_scatter(jnp.zeros((1 * lax.axis_size(('gx', 'gy')), 3, cell_coun...  322 us
    ppermute x8, starting transfers between devices, padded_2(): lax.ppermute(head, axis, [((i + 1) % count, i) for i in range(ends)])  32.8 us
    ppermute x8, starting transfers between devices, padded_2(): lax.ppermute(tail, axis, [(i, (i + 1) % count) for i in range(ends)])  22.3 us
    all_to_all x1, local copies, waits for them, and re-layouts, check_works_on(): jax.lax.all_to_all(jnp.stack([x0 for _ in range(jax.lax.axis_size(mesh_na...  16.1 us
    dot_general x2, matrix products, contact(): pull_vel = jnp.einsum('bqij,cbqj->cbi', kernel, near_vel, precision=highest)  11.6 us
    dot_general x2, matrix products, contact(): pull_pos = jnp.einsum('bqij,cbqj->cbi', kernel, near_pos, precision=highest)  11.2 us
    broadcast_in_dim x1, local copies, waits for them, and re-layouts, local(): jnp.zeros((1 * lax.axis_size(('gx', 'gy')), 3, cell_count), jnp.float32)  11 us
    ppermute x8, waiting for transfers between devices, padded_2(): lax.ppermute(tail, axis, [(i, (i + 1) % count) for i in range(ends)])  10.2 us
  transfers between devices with their start and end apart: 18, of which 6 were waited for; matrix products, arithmetic and copies ran while one was open for 7% of the time, Pallas kernels for 0%

profile of v1, /device:TPU:6, one launch (start us, length us, event | category | flops | bytes accessed | tf_op | source)
XLA Modules:
  0.0 482.4 jit_solution(9920169327509049612)
XLA Ops:
  8.8 6.8 %collective-permute-start.1 = (f32[7,16,128]{2,0,1:T(8,128)S(1)}, f32[7,16,128]{2,0,1:T(8,128)S(1)}, u32[]{:S(2)}, u32[]{:S(2)}) collective-permute-start(f32[7,16,128]{2,0,1:T(8,128)S(1)} %pad_maximum_fusion.5), channel_id=1, source_target_pairs={{1,0},{2,1},{3,2},{4,3},{5,4},{6,5},{7,6},{8,7},{9,8},{10,9},{11,1... | collective-permute-start | bytes 172040 | tf_op jit(solution)/shard_map/ppermute | solution.py:42
  15.6 1.9 collective-permute-start
  18.4 1.6 stack.3
  20.0 5.9 %all-to-all-start = ((f32[16,1,3,4096]{3,1,2,0:T(1,128)}), f32[16,1,3,4096]{3,1,2,0:T(1,128)S(1)}, u32[]{:S(2)}, u32[]{:S(2)}) async-start(f32[16,1,3,4096]{3,1,2,0:T(1,128)} %stack.3), calls=%async_computation | async-start | bytes 1572864 | tf_op jit(solution)/shard_map/all_to_all | solution.py:19
  26.7 2.0 collective-permute-start.5
  28.8 3.5 collective-permute-start.4
  37.8 2.2 fusion.2
  40.1 5.6 %fusion.49 = f32[3,16,128]{2,0,1:T(4,128)S(1)} fusion(f32[16,4,128]{2,1,0:T(4,128)S(1)} %bitcast.143, f32[16,128]{1,0:T(8,128)S(1)} %get-tuple-element.114, f32[16,4,128]{2,1,0:T(4,128)S(1)} %bitcast.146, f32[16,128]{1,0:T(8,128)S(1)} %get-tuple-element.113, f32[16,4,128]{2,1,0:T(4,128)S(1)} %bitcast.140, f32[16,128]{1,0:T(8,128)S(1)} %get-tuple-element.112, ...), kind=kOutput, calls=%fused_computation.55 | convolution fusion | flops 48277504 | bytes 311296 | tf_op jit(solution)/shard_map/while/body/eval_jaxpr/bqij,cbqj->cbi/dot_general | solution.py:58
  45.7 16.1 %copy.80 = f32[16,1,3,4096]{2,3,0,1:T(8,128)} copy(f32[16,1,3,4096]{3,1,2,0:T(1,128)S(1)} %all-to-all-done) | data formatting | bytes 1572864 | tf_op jit(solution)/shard_map/all_to_all | solution.py:19
  61.8 1.3 gather_fusion.1
  63.1 5.9 %multiply_reduce_fusion = (f32[3,16]{0,1:T(8,128)S(1)}, f32[3,16]{0,1:T(8,128)S(1)}, f32[3,16,128]{2,0,1:T(4,128)S(1)}, f32[3,16,128]{2,0,1:T(4,128)S(1)}) fusion(f32[16,128]{1,0:T(8,128)S(1)} %get-tuple-element.118, f32[3,16]{0,1:T(8,128)S(1)} %select_bitcast_fusion.1, f32[3,16,128]{2,1,0:T(8,128)S(1)} %copy-done.2, ...), kind=kOutput, calls=%fused_computation.142 | convolution fusion | flops 48351136 | bytes 401984 | tf_op jit(solution)/shard_map/while/body/eval_jaxpr/bqij,cbqj->cbi/dot_general | solution.py:59
  69.1 11.0 %broadcast_in_dim.105 = f32[16,3,4096]{1,2,0:T(8,128)} broadcast(f32[]{:T(128)} %constant.18.clone.1), dimensions={} | broadcast | bytes 786436 | tf_op jit(solution)/shard_map/broadcast_in_dim | solution.py:141
  80.2 2.2 scatter_fusion
  82.4 1.3 collective-permute-start.6
  83.7 4.5 collective-permute-start.7
  88.3 1.3 collective-permute-done.7
  89.7 1.9 collective-permute-start.9
  91.7 7.5 %collective-permute-start.8 = (f32[3,6,10,1]{3,2,1,0:T(8,128)S(1)}, f32[3,6,10,1]{3,2,1,0:T(8,128)S(1)}, u32[]{:S(2)}, u32[]{:S(2)}) collective-permute-start(f32[3,6,10,1]{3,2,1,0:T(8,128)S(1)} %get-tuple-element.78), channel_id=1, source_target_pairs={{1,0},{2,1},{3,2},{4,3},{5,4},{6,5},{7,6},{9,8},{10,9},{11,10},{12... | collective-permute-start | bytes 2168 | tf_op jit(solution)/shard_map/ppermute | solution.py:42
  99.3 3.9 collective-permute-start.3
  103.1 2.0 collective-permute-start.2
  105.6 8.0 %collective-permute-done.2 = f32[7,16,128]{2,0,1:T(8,128)S(1)} collective-permute-done((f32[7,16,128]{2,0,1:T(8,128)S(1)}, f32[7,16,128]{2,0,1:T(8,128)S(1)}, u32[]{:S(2)}, u32[]{:S(2)}) %collective-permute-start.2) | collective-permute-done | bytes 57376 | tf_op jit(solution)/shard_map/ppermute | solution.py:40
  114.5 322.4 %reduce-scatter.2.cloned.1.call-done = f32[1,3,4096]{1,2,0:T(8,128)} async-done(((f32[16,3,4096]{1,2,0:T(8,128)}), f32[1,3,4096]{1,2,0:T(8,128)}) %reduce-scatter.2.cloned.1.call-update) | async-done | bytes 49168 | tf_op jit(solution)/shard_map/reduce_scatter | solution.py:140
  436.9 2.2 copy.88
  439.3 2.5 collective-permute-start.10
  441.8 1.9 collective-permute-start.11
  443.8 2.3 fusion.5
  446.9 1.3 collective-permute-start.12
  448.2 4.5 collective-permute-start.13
  452.7 5.6 %fusion.57 = f32[3,16,128]{2,0,1:T(4,128)S(1)} fusion(f32[16,4,128]{2,1,0:T(4,128)S(1)} %bitcast.134, f32[16,128]{1,0:T(8,128)S(1)} %bitcast.152, f32[16,4,128]{2,1,0:T(4,128)S(1)} %bitcast.137, f32[16,128]{1,0:T(8,128)S(1)} %bitcast.155, f32[16,4,128]{2,1,0:T(4,128)S(1)} %bitcast.131, f32[16,128]{1,0:T(8,128)S(1)} %bitcast.149, ...), kind=kOutput, calls=%fused_computation.63 | convolution fusion | flops 48277504 | bytes 311296 | tf_op jit(solution)/shard_map/while/body/eval_jaxpr/bqij,cbqj->cbi/dot_general | solution.py:58
  458.5 3.4 collective-permute-start.15
  461.9 6.0 %collective-permute-start.14 = (f32[3,6,10,1]{3,2,1,0:T(8,128)S(1)}, f32[3,6,10,1]{3,2,1,0:T(8,128)S(1)}, u32[]{:S(2)}, u32[]{:S(2)}) collective-permute-start(f32[3,6,10,1]{3,2,1,0:T(8,128)S(1)} %get-tuple-element.76), channel_id=1, source_target_pairs={{1,0},{2,1},{3,2},{4,3},{5,4},{6,5},{7,6},{9,8},{10,9},{11,10},{12... | collective-permute-start | bytes 2168 | tf_op jit(solution)/shard_map/ppermute | solution.py:42
  467.9 5.6 %multiply_add_fusion = (f32[3,16,128]{2,0,1:T(4,128)S(1)}, f32[3,16,128]{2,0,1:T(4,128)S(1)}) fusion(f32[3,16,128]{2,0,1:T(4,128)S(1)} %get-tuple-element.106, f32[16,128]{1,0:T(8,128)S(1)} %get-tuple-element.117, f32[3,16,128]{2,0,1:T(4,128)S(1)} %get-tuple-element.119, f32[3,16]{0,1:T(8,128)S(1)} %select_bitcast_fusion.1, f32[3,16,128]{2,0,1:T(4,128)S(1)} %fusion.57, ...), kind=kOutput, calls=%fused_computation.144 | convolution fusion | flops 48320512 | bytes 393408 | tf_op jit(solution)/shard_map/while/body/eval_jaxpr/bqij,cbqj->cbi/dot_general | solution.py:59
  (70 shorter events, 13.5 us)
Async XLA Ops:
  7.2 32.9 %copy-start.1 = (f32[3,16,128]{2,1,0:T(8,128)S(1)}, f32[3,16,128]{2,1,0:T(8,128)}, u32[]{:S(2)}) copy-start(f32[3,16,128]{2,1,0:T(8,128)} %param.9) | copy-start | bytes 73732
  8.8 28.1 %collective-permute-start.1 = (f32[7,16,128]{2,0,1:T(8,128)S(1)}, f32[7,16,128]{2,0,1:T(8,128)S(1)}, u32[]{:S(2)}, u32[]{:S(2)}) collective-permute-start(f32[7,16,128]{2,0,1:T(8,128)S(1)} %pad_maximum_fusion.5), channel_id=1, source_target_pairs={{1,0},{2,1},{3,2},{4,3},{5,4},{6,5},{7,6},{8,7},{9,8},{10,9},{11,1... | collective-permute-start | bytes 172040 | tf_op jit(solution)/shard_map/ppermute | solution.py:42
  15.6 21.3 %collective-permute-start = (f32[7,16,128]{2,0,1:T(8,128)S(1)}, f32[7,16,128]{2,0,1:T(8,128)S(1)}, u32[]{:S(2)}, u32[]{:S(2)}) collective-permute-start(f32[7,16,128]{2,0,1:T(8,128)S(1)} %pad_maximum_fusion.5), channel_id=1, source_target_pairs={{0,1},{1,2},{2,3},{3,4},{4,5},{5,6},{6,7},{7,8},{8,9},{9,10},{10,1... | collective-permute-start | bytes 172040 | tf_op jit(solution)/shard_map/ppermute | solution.py:40
  20.0 25.7 %all-to-all-start = ((f32[16,1,3,4096]{3,1,2,0:T(1,128)}), f32[16,1,3,4096]{3,1,2,0:T(1,128)S(1)}, u32[]{:S(2)}, u32[]{:S(2)}) async-start(f32[16,1,3,4096]{3,1,2,0:T(1,128)} %stack.3), calls=%async_computation | async-start | bytes 1572864 | tf_op jit(solution)/shard_map/all_to_all | solution.py:19
  25.9 411.0 %reduce-scatter.2.cloned.1.call-start = ((), (), s32[]{:S(2)}) async-start(), calls=%async_computation.2 | async-start | bytes 35651584 | tf_op jit(solution)/shard_map/reduce_scatter | solution.py:140
  26.7 9.3 %collective-permute-start.5 = (f32[3,1,8,128]{3,2,1,0:T(8,128)S(1)}, f32[3,1,8,128]{3,2,1,0:T(8,128)S(1)}, u32[]{:S(2)}, u32[]{:S(2)}) collective-permute-start(f32[3,1,8,128]{3,2,1,0:T(8,128)S(1)} %get-tuple-element.105), channel_id=1, source_target_pairs={{0,32},{32,64},{64,96},{1,33},{33,65},{65,97},{2,34},{34,66},{66,9... | collective-permute-start | bytes 36872 | tf_op jit(solution)/shard_map/ppermute | solution.py:40
  28.8 8.1 %collective-permute-start.4 = (f32[3,1,8,128]{3,2,1,0:T(8,128)S(1)}, f32[3,1,8,128]{3,2,1,0:T(8,128)S(1)}, u32[]{:S(2)}, u32[]{:S(2)}) collective-permute-start(f32[3,1,8,128]{3,2,1,0:T(8,128)S(1)} %get-tuple-element.104), channel_id=1, source_target_pairs={{32,0},{64,32},{96,64},{33,1},{65,33},{97,65},{34,2},{66,34},{98,6... | collective-permute-start | bytes 36872 | tf_op jit(solution)/shard_map/ppermute | solution.py:42
  45.7 17.4 %copy-start.2 = (f32[3,16,128]{2,1,0:T(8,128)S(1)}, f32[3,16,128]{2,1,0:T(8,128)}, u32[]{:S(2)}) copy-start(f32[3,16,128]{2,1,0:T(8,128)} %param.10) | copy-start | bytes 73732
  82.4 356.8 %copy-start = (f32[3,4,8,128]{3,2,1,0:T(8,128)S(1)}, f32[3,4,8,128]{3,2,1,0:T(8,128)}, u32[]{:S(2)}) copy-start(f32[3,4,8,128]{3,2,1,0:T(8,128)} %param.17) | copy-start | bytes 147460
  82.4 5.9 %collective-permute-start.6 = (f32[3,6,1,128]{3,2,1,0:T(1,128)S(1)}, f32[3,6,1,128]{3,2,1,0:T(1,128)S(1)}, u32[]{:S(2)}, u32[]{:S(2)}) collective-permute-start(f32[3,6,1,128]{3,2,1,0:T(1,128)S(1)} %get-tuple-element.101), channel_id=1, source_target_pairs={{8,0},{16,8},{24,16},{9,1},{17,9},{25,17},{10,2},{18,10},{26,18},{... | collective-permute-start | bytes 27656 | tf_op jit(solution)/shard_map/ppermute | solution.py:42
  83.7 5.9 %collective-permute-start.7 = (f32[3,6,1,128]{3,2,1,0:T(1,128)S(1)}, f32[3,6,1,128]{3,2,1,0:T(1,128)S(1)}, u32[]{:S(2)}, u32[]{:S(2)}) collective-permute-start(f32[3,6,1,128]{3,2,1,0:T(1,128)S(1)} %get-tuple-element.100), channel_id=1, source_target_pairs={{0,8},{8,16},{16,24},{1,9},{9,17},{17,25},{2,10},{10,18},{18,26},{... | collective-permute-start | bytes 27656 | tf_op jit(solution)/shard_map/ppermute | solution.py:40
  89.7 349.4 %collective-permute-start.9 = (f32[3,6,10,1]{3,2,1,0:T(8,128)S(1)}, f32[3,6,10,1]{3,2,1,0:T(8,128)S(1)}, u32[]{:S(2)}, u32[]{:S(2)}) collective-permute-start(f32[3,6,10,1]{3,2,1,0:T(8,128)S(1)} %get-tuple-element.79), channel_id=1, source_target_pairs={{0,1},{1,2},{2,3},{3,4},{4,5},{5,6},{6,7},{8,9},{9,10},{10,11},{11... | collective-permute-start | bytes 2168 | tf_op jit(solution)/shard_map/ppermute | solution.py:40
  91.7 347.5 %collective-permute-start.8 = (f32[3,6,10,1]{3,2,1,0:T(8,128)S(1)}, f32[3,6,10,1]{3,2,1,0:T(8,128)S(1)}, u32[]{:S(2)}, u32[]{:S(2)}) collective-permute-start(f32[3,6,10,1]{3,2,1,0:T(8,128)S(1)} %get-tuple-element.78), channel_id=1, source_target_pairs={{1,0},{2,1},{3,2},{4,3},{5,4},{6,5},{7,6},{9,8},{10,9},{11,10},{12... | collective-permute-start | bytes 2168 | tf_op jit(solution)/shard_map/ppermute | solution.py:42
  99.3 6.4 %collective-permute-start.3 = (f32[7,16,128]{2,0,1:T(8,128)S(1)}, f32[7,16,128]{2,0,1:T(8,128)S(1)}, u32[]{:S(2)}, u32[]{:S(2)}) collective-permute-start(f32[7,16,128]{2,0,1:T(8,128)S(1)} %pad_maximum_fusion.4), channel_id=1, source_target_pairs={{1,0},{2,1},{3,2},{4,3},{5,4},{6,5},{7,6},{8,7},{9,8},{10,9},{11,1... | collective-permute-start | bytes 172040 | tf_op jit(solution)/shard_map/ppermute | solution.py:42
  103.1 10.4 %collective-permute-start.2 = (f32[7,16,128]{2,0,1:T(8,128)S(1)}, f32[7,16,128]{2,0,1:T(8,128)S(1)}, u32[]{:S(2)}, u32[]{:S(2)}) collective-permute-start(f32[7,16,128]{2,0,1:T(8,128)S(1)} %pad_maximum_fusion.4), channel_id=1, source_target_pairs={{0,1},{1,2},{2,3},{3,4},{4,5},{5,6},{6,7},{7,8},{8,9},{9,10},{10,1... | collective-permute-start | bytes 172040 | tf_op jit(solution)/shard_map/ppermute | solution.py:40
  439.3 6.7 %collective-permute-start.10 = (f32[3,1,8,128]{3,2,1,0:T(8,128)S(1)}, f32[3,1,8,128]{3,2,1,0:T(8,128)S(1)}, u32[]{:S(2)}, u32[]{:S(2)}) collective-permute-start(f32[3,1,8,128]{3,2,1,0:T(8,128)S(1)} %get-tuple-element.103), channel_id=1, source_target_pairs={{32,0},{64,32},{96,64},{33,1},{65,33},{97,65},{34,2},{66,34},{98,6... | collective-permute-start | bytes 36872 | tf_op jit(solution)/shard_map/ppermute | solution.py:42
  441.8 5.0 %collective-permute-start.11 = (f32[3,1,8,128]{3,2,1,0:T(8,128)S(1)}, f32[3,1,8,128]{3,2,1,0:T(8,128)S(1)}, u32[]{:S(2)}, u32[]{:S(2)}) collective-permute-start(f32[3,1,8,128]{3,2,1,0:T(8,128)S(1)} %get-tuple-element.102), channel_id=1, source_target_pairs={{0,32},{32,64},{64,96},{1,33},{33,65},{65,97},{2,34},{34,66},{66,9... | collective-permute-start | bytes 36872 | tf_op jit(solution)/shard_map/ppermute | solution.py:40
  446.9 11.5 %collective-permute-start.12 = (f32[3,6,1,128]{3,2,1,0:T(1,128)S(1)}, f32[3,6,1,128]{3,2,1,0:T(1,128)S(1)}, u32[]{:S(2)}, u32[]{:S(2)}) collective-permute-start(f32[3,6,1,128]{3,2,1,0:T(1,128)S(1)} %get-tuple-element.99), channel_id=1, source_target_pairs={{8,0},{16,8},{24,16},{9,1},{17,9},{25,17},{10,2},{18,10},{26,18},{... | collective-permute-start | bytes 27656 | tf_op jit(solution)/shard_map/ppermute | solution.py:42
  448.2 10.2 %collective-permute-start.13 = (f32[3,6,1,128]{3,2,1,0:T(1,128)S(1)}, f32[3,6,1,128]{3,2,1,0:T(1,128)S(1)}, u32[]{:S(2)}, u32[]{:S(2)}) collective-permute-start(f32[3,6,1,128]{3,2,1,0:T(1,128)S(1)} %get-tuple-element.98), channel_id=1, source_target_pairs={{0,8},{8,16},{16,24},{1,9},{9,17},{17,25},{2,10},{10,18},{18,26},{... | collective-permute-start | bytes 27656 | tf_op jit(solution)/shard_map/ppermute | solution.py:40
  458.5 16.3 %collective-permute-start.15 = (f32[3,6,10,1]{3,2,1,0:T(8,128)S(1)}, f32[3,6,10,1]{3,2,1,0:T(8,128)S(1)}, u32[]{:S(2)}, u32[]{:S(2)}) collective-permute-start(f32[3,6,10,1]{3,2,1,0:T(8,128)S(1)} %get-tuple-element.77), channel_id=1, source_target_pairs={{0,1},{1,2},{2,3},{3,4},{4,5},{5,6},{6,7},{8,9},{9,10},{10,11},{11... | collective-permute-start | bytes 2168 | tf_op jit(solution)/shard_map/ppermute | solution.py:40
  461.9 12.9 %collective-permute-start.14 = (f32[3,6,10,1]{3,2,1,0:T(8,128)S(1)}, f32[3,6,10,1]{3,2,1,0:T(8,128)S(1)}, u32[]{:S(2)}, u32[]{:S(2)}) collective-permute-start(f32[3,6,10,1]{3,2,1,0:T(8,128)S(1)} %get-tuple-element.76), channel_id=1, source_target_pairs={{1,0},{2,1},{3,2},{4,3},{5,4},{6,5},{7,6},{9,8},{10,9},{11,10},{12... | collective-permute-start | bytes 2168 | tf_op jit(solution)/shard_map/ppermute | solution.py:42
Sparse Core Ops, SparseCore 0:
  82.5 354.3 reduce-scatter.1
